TPU v7x, 256 devices: a whole 4x4x8 slice. The times are simulated.
256 devices in a mesh: ctx: 32 (over x, z), head: 8 (over y, core).
Axes of the slice: x: 4, y: 4, z: 8, core: 2. Of those that a mesh axis runs over, the one named last changes fastest.
Arguments:
- queries: bfloat16 [16384, 4096], P('ctx', 'head'), may hold values from -5 to 5
- key_rows: bfloat16 [16384, 1024], P('ctx', 'head'), may hold values from -5 to 5
- value_rows: bfloat16 [16384, 1024], P('ctx', 'head'), may hold values from -6 to 6
- slash_offsets: int32 [32, 4], P('head'), may hold values from 0 to 8, as said below
- union_blocks: int32 [8, 32, 2], P('head'), may hold values from 0 to 7, as said below
- head_picks: int32 [32, 32, 1], P('head'), may hold values from 0 to 1, as said below
- owner_counts: int32 [32, 32], P('head'), may hold values from 0 to 1, as said below
- out_weight: bfloat16 [4096, 4096], P(None, 'head'), may hold values from -0.09375 to 0.09375
Outputs:
- projected: bfloat16 [16384, 4096], P('ctx', 'head')
Inputs may be any that keep to these rules, and one draw needn't show every extreme that they name: `slash_offsets`: each head's offsets are distinct and include 0 and 8. `union_blocks`: the 2 entries of each KV head and sequence block are distinct. `head_picks`: the 1 entries of each query head and sequence block are distinct. `owner_counts`: equal to 1 for sequence block 0.
All inputs are finite; a program needn't handle non-finite values.
Results may differ from a plain program's by a relative error of at most 0.0056.
Values may be sent and summed in bfloat16 or wider, within the bound.
A program may use at most 128 MiB of HBM per device.

v0:
```python
import jax
import jax.numpy as jnp
from jax import lax
from jax.sharding import PartitionSpec as P

HEAD_SIZE = 128
BLOCK_TOKENS = 64
NS = 4
VPER = 1


def from_behind(array, axis, by):
    length = lax.axis_size(axis)
    pairs = [(i, i + by) for i in range(length) if 0 <= i + by < length]
    return lax.ppermute(array, axis, pairs)


def attend(
    vert_scores, vert_mask, diagonal_scores, slash_mask, vert_values, diagonal_values, per_dev
):
    masked_vert = jnp.where(vert_mask, vert_scores, -1e30)
    masked_slash = jnp.where(slash_mask, diagonal_scores, -1e30)
    peak = jnp.maximum(
        jnp.max(masked_vert, axis=-1, keepdims=True), jnp.max(masked_slash, axis=-1, keepdims=True)
    )
    weight_vert = jnp.exp(masked_vert - peak)
    weight_slash = jnp.exp(masked_slash - peak)
    total = jnp.sum(weight_vert, axis=-1, keepdims=True) + jnp.sum(
        weight_slash, axis=-1, keepdims=True
    )
    prob_vert = weight_vert.astype(jnp.bfloat16)
    slash_probability = weight_slash.astype(jnp.bfloat16).reshape(
        per_dev, BLOCK_TOKENS, NS, BLOCK_TOKENS
    )
    numer = jnp.dot(prob_vert, vert_values, preferred_element_type=jnp.float32)
    diagonal_portion = jnp.einsum(
        "wojf,wjfl->wol", slash_probability, diagonal_values, preferred_element_type=jnp.float32
    )
    numer = numer + diagonal_portion.reshape(per_dev * BLOCK_TOKENS, HEAD_SIZE)
    return (numer / total).astype(jnp.bfloat16)


def shards(
    queries, key_rows, value_rows, slash_offsets, union_blocks, head_picks, owner_counts, out_weight
):
    tokens = queries.shape[0]
    per_dev = tokens // BLOCK_TOKENS
    heads_here = slash_offsets.shape[0]
    groups_here = key_rows.shape[1] // HEAD_SIZE
    group_size = heads_here // groups_here
    owners = lax.axis_size("ctx")
    device_rank = lax.axis_index("ctx")
    scale_of_scores = jnp.float32(HEAD_SIZE ** (-0.5))
    stacked = jnp.stack([key_rows, value_rows])
    previous = from_behind(stacked, "ctx", 1)
    extended = jnp.concatenate([previous, stacked], axis=1).reshape(
        2, 2 * per_dev, BLOCK_TOKENS, groups_here, HEAD_SIZE
    )
    local_blocks = stacked.reshape(2, per_dev, BLOCK_TOKENS, groups_here, HEAD_SIZE)
    head_group = jnp.arange(heads_here, dtype=jnp.int32) // group_size
    mine_union = lax.dynamic_index_in_dim(union_blocks, device_rank, 1, keepdims=False)
    owner_base = jnp.arange(owners, dtype=jnp.int32)[:, None] * per_dev
    slot_rank = jnp.arange(VPER, dtype=jnp.int32)
    chosen = slot_rank[None, None, :] < owner_counts[:, :, None]
    mine_picks = lax.dynamic_index_in_dim(head_picks, device_rank, 1, keepdims=False)
    chosen_local = jnp.take_along_axis(mine_union[head_group], mine_picks, axis=1)
    block_rows = local_blocks[:, chosen_local, :, head_group[:, None], :]
    gathered = lax.all_gather(block_rows[:, None], "ctx", axis=1, tiled=True)
    slot_block = owner_base[None] + jnp.take_along_axis(
        union_blocks[head_group], head_picks, axis=2
    )
    source_of = list(range(heads_here))
    query_place = device_rank * tokens + jnp.arange(tokens, dtype=jnp.int32)
    query_block = device_rank * per_dev + jnp.arange(per_dev, dtype=jnp.int32)
    inner_offset = jnp.arange(BLOCK_TOKENS, dtype=jnp.int32)
    local_index = jnp.arange(per_dev, dtype=jnp.int32)
    per_head = []
    for head_index in range(heads_here):
        kv_index = head_index // group_size
        offsets = slash_offsets[head_index]
        query_head = queries[:, head_index * HEAD_SIZE : (head_index + 1) * HEAD_SIZE]
        vertical = gathered[source_of[head_index]]
        blocks_flat = slot_block[head_index].reshape(-1)
        valid_flat = chosen[head_index].reshape(-1)
        slot_count = blocks_flat.shape[0]
        vert_keys = vertical[:, :, 0].reshape(slot_count * BLOCK_TOKENS, HEAD_SIZE)
        vert_values = vertical[:, :, 1].reshape(slot_count * BLOCK_TOKENS, HEAD_SIZE)
        vert_scores = (
            jnp.einsum("qd,kd->qk", query_head, vert_keys, preferred_element_type=jnp.float32)
            * scale_of_scores
        )
        distance = query_block[:, None] - blocks_flat[None, :]
        on_slash = jnp.any(distance[:, :, None] == offsets[None, None, :], axis=2)
        block_mask = valid_flat[None, :] & jnp.logical_not(on_slash)
        key_place = (blocks_flat[:, None] * BLOCK_TOKENS + inner_offset[None, :]).reshape(-1)
        vert_mask = jnp.broadcast_to(
            block_mask[:, None, :, None], (per_dev, BLOCK_TOKENS, slot_count, BLOCK_TOKENS)
        ).reshape(tokens, slot_count * BLOCK_TOKENS)
        vert_mask = vert_mask & (key_place[None, :] <= query_place[:, None])
        group_slab = extended[:, :, :, kv_index, :]
        ext_index = local_index[:, None] + per_dev - offsets[None, :]
        slash_rows = group_slab[:, ext_index]
        diagonal_scores = (
            jnp.einsum(
                "hax,hisx->hais",
                query_head.reshape(per_dev, BLOCK_TOKENS, HEAD_SIZE),
                slash_rows[0],
                preferred_element_type=jnp.float32,
            )
            * scale_of_scores
        )
        slash_valid = query_block[:, None] - offsets[None, :] >= 0
        slash_mask = slash_valid[:, None, :, None] & (
            (offsets[None, None, :, None] > 0)
            | (inner_offset[None, None, None, :] <= inner_offset[None, :, None, None])
        )
        slash_mask = slash_mask.reshape(tokens, NS * BLOCK_TOKENS)
        per_head.append(
            attend(
                vert_scores,
                vert_mask,
                diagonal_scores.reshape(tokens, NS * BLOCK_TOKENS),
                slash_mask,
                vert_values,
                slash_rows[1],
                per_dev,
            )
        )
    attended = jnp.concatenate(per_head, axis=1)
    projected = jnp.dot(
        lax.all_gather(attended, "head", axis=1, tiled=True),
        out_weight,
        preferred_element_type=jnp.float32,
    )
    return projected.astype(jnp.bfloat16)


def solution(mesh):
    in_specs = (
        P("ctx", "head"),
        P("ctx", "head"),
        P("ctx", "head"),
        P("head", None),
        P("head", None, None),
        P("head", None, None),
        P("head", None),
        P(None, "head"),
    )
    out_specs = P("ctx", "head")
    return jax.shard_map(shards, mesh=mesh, in_specs=in_specs, out_specs=out_specs, check_vma=False)
```

profile of v0, /device:TPU:1, one launch (start us, length us, event | category | flops | bytes accessed | tf_op | source)
XLA Modules:
  0.0 189.1 jit_solution(1846127941252690670)
XLA Ops:
  6.5 0.8 constant_dynamic-slice_fusion
  7.5 0.9 dynamic-slice_reduce_fusion
  8.4 0.6 gather_fusion.6
  9.1 1.0 pad_maximum_fusion.1
  10.1 1.2 gather_fusion
  11.4 1.0 pad_maximum_fusion.2
  12.4 4.4 %collective-permute-start = (bf16[2,512,128]{2,1,0:T(8,128)(2,1)S(1)}, bf16[2,512,128]{2,1,0:T(8,128)(2,1)S(1)}, u32[]{:S(2)}, u32[]{:S(2)}) collective-permute-start(bf16[2,512,128]{2,1,0:T(8,128)(2,1)S(1)} %pad_maximum_fusion.2), channel_id=1, source_target_pairs={{0,8},{8,16},{16,24},{24,32},{32,40},{40,48},{48,56},{56,64},{64,7... | collective-permute-start | bytes 786440 | tf_op jit(solution)/shard_map/ppermute | solution.py:15
  16.8 0.7 fusion.89
  17.6 0.8 copy.55
  18.3 1.5 gather_fusion.5
  20.8 0.7 subtract_compare_fusion.3
  21.6 0.8 broadcast_or_fusion.3
  23.1 0.6 broadcast_in_dim.29
  23.7 4.7 %reshape.1051 = pred[512,2048]{0,1:T(32,128)(4,1)} reshape(pred[8,64,32,64]{1,0,3,2:T(8,128)(4,1)S(1)} %broadcast_in_dim.29) | data formatting | bytes 2097152 | tf_op jit(solution)/shard_map/reshape | solution.py:98
  28.4 0.7 add.293
  29.2 0.6 broadcast_in_dim.33
  29.8 4.7 %reshape.1054 = pred[512,2048]{0,1:T(32,128)(4,1)} reshape(pred[8,64,32,64]{1,0,3,2:T(8,128)(4,1)S(1)} %broadcast_in_dim.33) | data formatting | bytes 2097152 | tf_op jit(solution)/shard_map/reshape | solution.py:98
  34.5 0.7 add.307
  35.3 0.6 broadcast_in_dim.34
  35.9 4.7 %reshape.1057 = pred[512,2048]{0,1:T(32,128)(4,1)} reshape(pred[8,64,32,64]{1,0,3,2:T(8,128)(4,1)S(1)} %broadcast_in_dim.34) | data formatting | bytes 2097152 | tf_op jit(solution)/shard_map/reshape | solution.py:98
  40.6 0.7 add.314
  42.0 4.7 %reshape.1060 = pred[512,2048]{0,1:T(32,128)(4,1)} reshape(pred[8,64,32,64]{1,0,3,2:T(8,128)(4,1)S(1)} %broadcast_in_dim.35) | data formatting | bytes 2097152 | tf_op jit(solution)/shard_map/reshape | solution.py:98
  46.7 0.7 add.321
  47.4 0.7 fusion.99
  48.2 0.7 gather_fusion.1
  49.1 1.0 copy-done.9
  50.0 1.3 fusion.107
  51.5 0.7 gather_fusion.2
  52.3 1.0 copy-done.8
  53.7 0.6 reduce_max.94
  54.4 0.7 gather_fusion.3
  55.2 1.0 copy-done.7
  56.6 0.7 reduce_max.98
  57.2 1.7 gather_fusion.4
  58.9 1.3 copy.70
  60.2 1.0 copy-done.5
  61.6 32.7 %all-gather.6.cloned.1.call-done = bf16[4,64,64,128]{3,2,1,0:T(8,128)(2,1)} async-done(((bf16[4,2,64,128]{3,2,1,0:T(8,128)(2,1)}), bf16[4,64,64,128]{3,2,1,0:T(8,128)(2,1)}) %all-gather.6.cloned.1.call-update) | async-done | bytes 4194320 | tf_op jit(solution)/shard_map/all_gather | solution.py:68
  94.4 4.4 %fusion.94 = (bf16[1,64,64,128]{3,2,1,0:T(8,128)(2,1)S(1)}, bf16[1,64,64,128]{3,2,1,0:T(8,128)(2,1)}, bf16[1,64,64,128]{3,2,1,0:T(8,128)(2,1)}, bf16[1,64,64,128]{3,2,1,0:T(8,128)(2,1)}) fusion(bf16[4,64,64,128]{3,2,1,0:T(8,128)(2,1)} %all-gather.6.cloned.1.call-done), kind=kLoop, calls=%fused_computation.176 | loop fusion | bytes 8388608 | tf_op jit(solution)/shard_map/slice | solution.py:82
  98.7 0.9 fusion.95
  99.6 3.6 %fusion.106 = (f32[512]{0:T(512)S(1)}, f32[512,2048]{0,1:T(8,128)}) fusion(bf16[2048,128]{1,0:T(8,128)(2,1)S(1)} %bitcast.252, bf16[512,512]{1,0:T(8,128)(2,1)} %param.8, pred[512,2048]{0,1:T(32,128)(4,1)S(1)} %copy-done.19, s32[512]{0:T(512)S(1)} %copy-done.37, s32[2048]{0:T(1024)S(1)} %copy-done.32), kind=kOutput, calls=%fused_computation.188 | convolution fusion | flops 273677824 | bytes 5910528 | tf_op jit(solution)/shard_map/qd,kd->qk/dot_general | solution.py:89
  103.3 1.5 fusion.64
  104.8 1.7 fusion.78
  106.5 2.1 %fusion.96 = (bf16[32,1,1,64,128]{4,3,2,0,1:T(8,128)(2,1)}, bf16[32,1,1,64,128]{4,3,2,0,1:T(8,128)(2,1)S(1)}) fusion(bf16[32,1,2,64,128]{4,3,2,0,1:T(8,128)(2,1)} %bitcast.227), kind=kLoop, calls=%fused_computation.178 | loop fusion | bytes 2097152 | tf_op jit(solution)/shard_map/slice | solution.py:87
  108.6 3.6 %fusion.104 = (f32[512]{0:T(512)S(1)}, f32[512,2048]{0,1:T(8,128)}) fusion(bf16[2048,128]{1,0:T(8,128)(2,1)S(1)} %bitcast.253, bf16[512,512]{1,0:T(8,128)(2,1)} %param.8, pred[512,2048]{0,1:T(32,128)(4,1)S(1)} %copy-done.18, s32[512]{0:T(512)S(1)} %copy-done.37, s32[2048]{0:T(1024)S(1)} %copy-done.31), kind=kOutput, calls=%fused_computation.186 | convolution fusion | flops 273677824 | bytes 5910528 | tf_op jit(solution)/shard_map/qd,kd->qk/dot_general | solution.py:89
  112.5 2.2 %fusion.76 = f32[8,64,128,1]{2,1,3,0:T(8,128)} fusion(f32[8,64,4,64]{1,3,2,0:T(8,128)S(1)} %get-tuple-element.68, bf16[2,8,4,64,128]{4,3,2,1,0:T(8,128)(2,1)} %bitcast.234, f32[8,64]{1,0:T(8,128)S(1)} %max.47), kind=kOutput, calls=%fused_computation.70 | convolution fusion | flops 33816576 | bytes 1312768 | tf_op jit(solution)/shard_map/wojf,wjfl->wol/dot_general | solution.py:36
  114.7 2.1 %fusion.97 = (bf16[32,1,1,64,128]{4,3,2,0,1:T(8,128)(2,1)}, bf16[32,1,1,64,128]{4,3,2,0,1:T(8,128)(2,1)S(1)}) fusion(bf16[32,1,2,64,128]{4,3,2,0,1:T(8,128)(2,1)} %bitcast.226), kind=kLoop, calls=%fused_computation.179 | loop fusion | bytes 2097152 | tf_op jit(solution)/shard_map/slice | solution.py:87
  116.8 3.7 %fusion.102 = (f32[512]{0:T(512)S(1)}, f32[512,2048]{0,1:T(8,128)}) fusion(bf16[2048,128]{1,0:T(8,128)(2,1)S(1)} %bitcast.254, bf16[512,512]{1,0:T(8,128)(2,1)} %param.8, pred[512,2048]{0,1:T(32,128)(4,1)S(1)} %copy-done.17, s32[512]{0:T(512)S(1)} %copy-done.37, s32[2048]{0:T(1024)S(1)} %copy-done.30), kind=kOutput, calls=%fused_computation.184 | convolution fusion | flops 273677824 | bytes 5910528 | tf_op jit(solution)/shard_map/qd,kd->qk/dot_general | solution.py:89
  120.8 2.2 %fusion.74 = f32[8,64,128,1]{2,1,3,0:T(8,128)} fusion(f32[8,64,4,64]{1,3,2,0:T(8,128)S(1)} %get-tuple-element.64, bf16[2,8,4,64,128]{4,3,2,1,0:T(8,128)(2,1)} %bitcast.232, f32[8,64]{1,0:T(8,128)S(1)} %max.49), kind=kOutput, calls=%fused_computation.69 | convolution fusion | flops 33816576 | bytes 1312768 | tf_op jit(solution)/shard_map/wojf,wjfl->wol/dot_general | solution.py:36
  122.9 0.9 fusion.98
  123.9 3.7 %fusion.100 = (f32[512]{0:T(512)S(1)}, f32[512,2048]{0,1:T(8,128)}) fusion(bf16[2048,128]{1,0:T(8,128)(2,1)S(1)} %bitcast.251, bf16[512,512]{1,0:T(8,128)(2,1)} %param.8, pred[512,2048]{0,1:T(32,128)(4,1)S(1)} %copy-done.16, s32[512]{0:T(512)S(1)} %copy-done.37, s32[2048]{0:T(1024)S(1)} %copy-done.29), kind=kOutput, calls=%fused_computation.182 | convolution fusion | flops 273677824 | bytes 5910528 | tf_op jit(solution)/shard_map/qd,kd->qk/dot_general | solution.py:89
  129.1 3.0 %fusion = f32[512]{0:T(512)S(1)} fusion(f32[512,2048]{0,1:T(8,128)} %get-tuple-element.70, f32[512]{0:T(512)S(1)} %max.44), kind=kLoop, calls=%fused_computation.15 | loop fusion | flops 2096640 | bytes 4198400 | tf_op jit(solution)/shard_map/reduce_sum | solution.py:28
  132.6 0.6 fusion.2
  133.2 0.6 copy-done.2
  133.8 0.6 fusion.4
  134.5 0.8 copy-done.3
  135.3 0.6 fusion.6
  135.9 0.6 copy-done
  136.5 0.8 fusion.61
  137.3 0.7 fusion.58
  138.1 0.8 fusion.55
  138.8 0.8 fusion.52
  139.6 0.8 pad_maximum_fusion
  140.5 35.2 %all-gather.4.cloned.1.call-done = bf16[512,4096]{0,1:T(8,128)(2,1)} async-done(((bf16[512,512]{0,1:T(8,128)(2,1)}), bf16[512,4096]{0,1:T(8,128)(2,1)}) %all-gather.4.cloned.1.call-update) | async-done | bytes 4194320 | tf_op jit(solution)/shard_map/all_gather | solution.py:131
  175.7 6.6 %convolution_convert_fusion = bf16[512,512]{1,0:T(8,128)(2,1)} fusion(bf16[512,4096]{0,1:T(8,128)(2,1)} %all-gather.4.cloned.1.call-done, bf16[4096,512]{1,0:T(8,128)(2,1)} %param.15), kind=kOutput, calls=%fused_computation.43 | convolution fusion | flops 2147745792 | bytes 8912896 | tf_op jit(solution)/shard_map/dot_general | solution.py:130
  (170 shorter events, 7.1 us)
Async XLA Ops:
  6.5 13.9 %copy-start.28 = (s32[4,32,1]{1,2,0:T(1,128)S(1)}, s32[4,32,1]{1,2,0:T(1,128)}, u32[]{:S(2)}) copy-start(s32[4,32,1]{1,2,0:T(1,128)} %param.13) | copy-start | bytes 1540
  6.5 13.4 %copy-start.35 = (s32[4,4]{1,0:T(4,128)S(1)}, s32[4,4]{1,0:T(4,128)}, u32[]{:S(2)}) copy-start(s32[4,4]{1,0:T(4,128)} %param.11) | copy-start | bytes 196
  6.5 14.2 %copy-start.36 = (s32[4,32]{1,0:T(4,128)S(1)}, s32[4,32]{1,0:T(4,128)}, u32[]{:S(2)}) copy-start(s32[4,32]{1,0:T(4,128)} %param.14) | copy-start | bytes 1540
  6.5 87.8 %all-gather.6.cloned.1.call-start = ((), (), s32[]{:S(2)}) async-start(), calls=%async_computation.1 | async-start | bytes 4325376 | tf_op jit(solution)/shard_map/all_gather | solution.py:68
  11.3 164.4 %all-gather.4.cloned.1.call-start = ((), (), s32[]{:S(2)}) async-start(), calls=%async_computation | async-start | bytes 4718592 | tf_op jit(solution)/shard_map/all_gather | solution.py:131
  12.4 35.8 %collective-permute-start = (bf16[2,512,128]{2,1,0:T(8,128)(2,1)S(1)}, bf16[2,512,128]{2,1,0:T(8,128)(2,1)S(1)}, u32[]{:S(2)}, u32[]{:S(2)}) collective-permute-start(bf16[2,512,128]{2,1,0:T(8,128)(2,1)S(1)} %pad_maximum_fusion.2), channel_id=1, source_target_pairs={{0,8},{8,16},{16,24},{24,32},{32,40},{40,48},{48,56},{56,64},{64,7... | collective-permute-start | bytes 786440 | tf_op jit(solution)/shard_map/ppermute | solution.py:15
  35.9 11.5 %copy-start.22 = (bf16[512,512]{1,0:T(8,128)(2,1)S(1)}, bf16[512,512]{1,0:T(8,128)(2,1)}, u32[]{:S(2)}) copy-start(bf16[512,512]{1,0:T(8,128)(2,1)} %param.8) | copy-start | bytes 1572868
  35.9 12.2 %copy-start.14 = (bf16[512,128]{1,0:T(8,128)(2,1)S(1)}, bf16[512,128]{1,0:T(8,128)(2,1)}, u32[]{:S(2)}) copy-start(bf16[512,128]{1,0:T(8,128)(2,1)} %param.10) | copy-start | bytes 393220
  35.9 12.2 %copy-start.15 = (bf16[512,128]{1,0:T(8,128)(2,1)S(1)}, bf16[512,128]{1,0:T(8,128)(2,1)}, u32[]{:S(2)}) copy-start(bf16[512,128]{1,0:T(8,128)(2,1)} %param.9) | copy-start | bytes 393220
  46.7 3.3 %copy-start.27 = (pred[64,4,64]{0,2,1:T(8,128)(4,1)S(1)}, pred[64,4,64]{0,2,1:T(8,128)(4,1)}, u32[]{:S(2)}) copy-start(pred[64,4,64]{0,2,1:T(8,128)(4,1)} %get-tuple-element.21) | copy-start | bytes 49156
  46.7 3.3 %copy-start.41 = (pred[8,4]{1,0:T(8,128)(4,1)S(1)}, pred[8,4]{1,0:T(8,128)(4,1)}, u32[]{:S(2)}) copy-start(pred[8,4]{1,0:T(8,128)(4,1)} %get-tuple-element.49) | copy-start | bytes 100
  49.0 4.4 %copy-start.26 = (pred[64,4,64]{0,2,1:T(8,128)(4,1)S(1)}, pred[64,4,64]{0,2,1:T(8,128)(4,1)}, u32[]{:S(2)}) copy-start(pred[64,4,64]{0,2,1:T(8,128)(4,1)} %get-tuple-element.22) | copy-start | bytes 49156
  49.0 4.4 %copy-start.40 = (pred[8,4]{1,0:T(8,128)(4,1)S(1)}, pred[8,4]{1,0:T(8,128)(4,1)}, u32[]{:S(2)}) copy-start(pred[8,4]{1,0:T(8,128)(4,1)} %get-tuple-element.50) | copy-start | bytes 100
  49.1 1.0 copy-start.9
  52.2 4.0 %copy-start.23 = (bf16[512,128]{1,0:T(8,128)(2,1)S(1)}, bf16[512,128]{1,0:T(8,128)(2,1)}, u32[]{:S(2)}) copy-start(bf16[512,128]{1,0:T(8,128)(2,1)} %get-tuple-element.20) | copy-start | bytes 393220
  52.2 4.0 %copy-start.25 = (pred[64,4,64]{0,2,1:T(8,128)(4,1)S(1)}, pred[64,4,64]{0,2,1:T(8,128)(4,1)}, u32[]{:S(2)}) copy-start(pred[64,4,64]{0,2,1:T(8,128)(4,1)} %get-tuple-element.23) | copy-start | bytes 49156
  52.2 4.0 %copy-start.39 = (pred[8,4]{1,0:T(8,128)(4,1)S(1)}, pred[8,4]{1,0:T(8,128)(4,1)}, u32[]{:S(2)}) copy-start(pred[8,4]{1,0:T(8,128)(4,1)} %get-tuple-element.51) | copy-start | bytes 100
  52.3 1.0 copy-start.8
  55.1 6.1 %copy-start.24 = (pred[64,4,64]{0,2,1:T(8,128)(4,1)S(1)}, pred[64,4,64]{0,2,1:T(8,128)(4,1)}, u32[]{:S(2)}) copy-start(pred[64,4,64]{0,2,1:T(8,128)(4,1)} %get-tuple-element.24) | copy-start | bytes 49156
  55.1 6.1 %copy-start.38 = (pred[8,4]{1,0:T(8,128)(4,1)S(1)}, pred[8,4]{1,0:T(8,128)(4,1)}, u32[]{:S(2)}) copy-start(pred[8,4]{1,0:T(8,128)(4,1)} %get-tuple-element.52) | copy-start | bytes 100
  55.2 1.0 copy-start.7
  60.2 1.0 copy-start.5
  61.6 38.0 %copy-start.32 = (s32[2048]{0:T(1024)S(1)}, s32[2048]{0:T(1024)}, u32[]{:S(2)}) copy-start(s32[2048]{0:T(1024)} %add.293) | copy-start | bytes 24580
  61.6 38.0 %copy-start.37 = (s32[512]{0:T(512)S(1)}, s32[512]{0:T(512)}, u32[]{:S(2)}) copy-start(s32[512]{0:T(512)} %iota_add_fusion.4) | copy-start | bytes 6148
  94.4 5.3 %copy-start.19 = (pred[512,2048]{0,1:T(32,128)(4,1)S(1)}, pred[512,2048]{0,1:T(32,128)(4,1)}, u32[]{:S(2)}) copy-start(pred[512,2048]{0,1:T(32,128)(4,1)} %reshape.1051) | copy-start | bytes 3145732
  99.6 8.9 %copy-start.31 = (s32[2048]{0:T(1024)S(1)}, s32[2048]{0:T(1024)}, u32[]{:S(2)}) copy-start(s32[2048]{0:T(1024)} %add.307) | copy-start | bytes 24580
  103.3 5.3 %copy-start.18 = (pred[512,2048]{0,1:T(32,128)(4,1)S(1)}, pred[512,2048]{0,1:T(32,128)(4,1)}, u32[]{:S(2)}) copy-start(pred[512,2048]{0,1:T(32,128)(4,1)} %reshape.1054) | copy-start | bytes 3145732
  108.6 8.2 %copy-start.30 = (s32[2048]{0:T(1024)S(1)}, s32[2048]{0:T(1024)}, u32[]{:S(2)}) copy-start(s32[2048]{0:T(1024)} %add.314) | copy-start | bytes 24580
  112.3 4.5 %copy-start.17 = (pred[512,2048]{0,1:T(32,128)(4,1)S(1)}, pred[512,2048]{0,1:T(32,128)(4,1)}, u32[]{:S(2)}) copy-start(pred[512,2048]{0,1:T(32,128)(4,1)} %reshape.1057) | copy-start | bytes 3145732
  116.8 6.2 %copy-start.4 = (bf16[1,64,64,128]{3,2,1,0:T(8,128)(2,1)S(1)}, bf16[1,64,64,128]{3,2,1,0:T(8,128)(2,1)}, u32[]{:S(2)}) copy-start(bf16[1,64,64,128]{3,2,1,0:T(8,128)(2,1)} %get-tuple-element.8) | copy-start | bytes 3145732
  116.8 7.0 %copy-start.29 = (s32[2048]{0:T(1024)S(1)}, s32[2048]{0:T(1024)}, u32[]{:S(2)}) copy-start(s32[2048]{0:T(1024)} %add.321) | copy-start | bytes 24580
  120.6 3.3 %copy-start.16 = (pred[512,2048]{0,1:T(32,128)(4,1)S(1)}, pred[512,2048]{0,1:T(32,128)(4,1)}, u32[]{:S(2)}) copy-start(pred[512,2048]{0,1:T(32,128)(4,1)} %reshape.1060) | copy-start | bytes 3145732
  123.8 4.0 %copy-start.6 = (bf16[32,2,64,128]{3,2,0,1:T(8,128)(2,1)S(1)}, bf16[32,2,64,128]{3,2,0,1:T(8,128)(2,1)}, u32[]{:S(2)}) copy-start(bf16[32,2,64,128]{3,2,0,1:T(8,128)(2,1)} %copy-done.5) | copy-start | bytes 3145732
  123.8 4.6 %copy-start.33 = (f32[512]{0:T(512)S(1)}, f32[512]{0:T(512)}, u32[]{:S(2)}) copy-start(f32[512]{0:T(512)} %reduce_max.94) | copy-start | bytes 6148
  123.8 4.7 %copy-start.20 = (f32[8,64,128,1]{2,1,3,0:T(8,128)S(1)}, f32[8,64,128,1]{2,1,3,0:T(8,128)}, u32[]{:S(2)}) copy-start(f32[8,64,128,1]{2,1,3,0:T(8,128)} %fusion.76) | copy-start | bytes 786436
  123.8 4.8 %copy-start.34 = (f32[512]{0:T(512)S(1)}, f32[512]{0:T(512)}, u32[]{:S(2)}) copy-start(f32[512]{0:T(512)} %reduce_max.98) | copy-start | bytes 6148
  123.9 4.9 %copy-start.21 = (f32[8,64,128,1]{2,1,3,0:T(8,128)S(1)}, f32[8,64,128,1]{2,1,3,0:T(8,128)}, u32[]{:S(2)}) copy-start(f32[8,64,128,1]{2,1,3,0:T(8,128)} %fusion.74) | copy-start | bytes 786436
  128.9 6.9 %copy-start.10 = (bf16[32,1,1,64,128]{4,3,2,0,1:T(8,128)(2,1)S(1)}, bf16[32,1,1,64,128]{4,3,2,0,1:T(8,128)(2,1)}, u32[]{:S(2)}) copy-start(bf16[32,1,1,64,128]{4,3,2,0,1:T(8,128)(2,1)} %get-tuple-element.9) | copy-start | bytes 1572868
  129.1 3.5 %copy-start.1 = (f32[512,2048]{0,1:T(8,128)S(1)}, f32[512,2048]{0,1:T(8,128)}, u32[]{:S(2)}) copy-start(f32[512,2048]{0,1:T(8,128)} %get-tuple-element.66) | copy-start | bytes 12582916
  129.1 4.7 %copy-start.2 = (f32[512,2048]{0,1:T(8,128)S(1)}, f32[512,2048]{0,1:T(8,128)}, u32[]{:S(2)}) copy-start(f32[512,2048]{0,1:T(8,128)} %get-tuple-element.62) | copy-start | bytes 12582916
  132.6 2.7 %copy-start.3 = (f32[512,2048]{0,1:T(8,128)S(1)}, f32[512,2048]{0,1:T(8,128)}, u32[]{:S(2)}) copy-start(f32[512,2048]{0,1:T(8,128)} %get-tuple-element.58) | copy-start | bytes 12582916
  133.8 2.7 %copy-start = (f32[512,2048]{0,1:T(8,128)S(1)}, f32[512,2048]{0,1:T(8,128)}, u32[]{:S(2)}) copy-start(f32[512,2048]{0,1:T(8,128)} %get-tuple-element.70) | copy-start | bytes 12582916
  135.3 2.0 %copy-start.11 = (bf16[32,1,1,64,128]{4,3,2,0,1:T(8,128)(2,1)S(1)}, bf16[32,1,1,64,128]{4,3,2,0,1:T(8,128)(2,1)}, u32[]{:S(2)}) copy-start(bf16[32,1,1,64,128]{4,3,2,0,1:T(8,128)(2,1)} %get-tuple-element.11) | copy-start | bytes 1572868
  136.5 1.5 copy-start.12
  137.3 1.5 copy-start.13
Sparse Core Ops, SparseCore 0:
  11.4 82.9 all-gather.5
  140.6 35.0 all-gather.3
where the time goes:
time: 190 us; the launch traced here: 189 us
  waiting for transfers between devices  68 us (36%)
  local copies, waits for them, and re-layouts  56.4 us (30%)
  matrix products  33.1 us (17%)
  between operations  14.1 us (7%)
  other arithmetic  13.2 us (7%)
  starting transfers between devices  4.43 us (2%)
    all_gather x1, waiting for transfers between devices, shards(): lax.all_gather(attended, 'head', axis=1, tiled=True)  35.2 us
    all_gather x1, waiting for transfers between devices, shards(): gathered = lax.all_gather(block_rows[:, None], 'ctx', axis=1, tiled=True)  32.7 us
    reshape x4, local copies, waits for them, and re-layouts, shards(): vert_mask = jnp.broadcast_to(block_mask[:, None, :, None], (per_dev, BLOC...  18.9 us
    dot_general x4, matrix products, shards(): jnp.einsum('qd,kd->qk', query_head, vert_keys, preferred_element_type=jnp...  14.6 us
    unnamed x88, local copies, waits for them, and re-layouts  6.68 us
    dot_general x1, matrix products, shards(): jnp.dot(lax.all_gather(attended, 'head', axis=1, tiled=True), out_weight,...  6.61 us
    dot_general x4, matrix products, attend(): jnp.einsum('wojf,wjfl->wol', slash_probability, diagonal_values, preferre...  6.35 us
    slice x4, local copies, waits for them, and re-layouts, shards(): vertical[:, :, 1].reshape(slot_count * BLOCK_TOKENS, HEAD_SIZE)  5.9 us
  transfers between devices with their start and end apart: 3, of which 2 were waited for; matrix products, arithmetic and copies ran while one was open for 22% of the time, Pallas kernels for 0%

commit v1 on v0

--- a/solution.py
+++ b/solution.py
@@ -7,6 +7,12 @@
 BLOCK_TOKENS = 64
 NS = 4
 VPER = 1
+
+
+def tiled_gather(x, axis, dim):
+    peers = lax.axis_size(axis)
+    repeats = [peers if d == dim else 1 for d in range(x.ndim)]
+    return lax.all_to_all(jnp.tile(x, repeats), axis, split_axis=dim, concat_axis=dim, tiled=True)
 
 
 def from_behind(array, axis, by):
@@ -128,9 +134,7 @@
         )
     attended = jnp.concatenate(per_head, axis=1)
     projected = jnp.dot(
-        lax.all_gather(attended, "head", axis=1, tiled=True),
-        out_weight,
-        preferred_element_type=jnp.float32,
+        tiled_gather(attended, "head", 1), out_weight, preferred_element_type=jnp.float32
     )
     return projected.astype(jnp.bfloat16)
 

time: 190 us -> 218 us (1.15)
  blocking collectives: 0 us -> 56.8 us
  waiting for transfers between devices: 68 us -> 32.8 us
  local copies, waits for them, and re-layouts: 56.4 us -> 63.4 us
    all_to_all x0 -> x1, blocking collectives: none -> 56.8 us  [tiled_gather(): lax.all_to_all(jnp.tile(x, repeats), axis, split_axis=dim, concat_axis=di...]
    all_gather x1 -> x0, waiting for transfers between devices: 35.2 us -> none  [shards(): lax.all_gather(attended, 'head', axis=1, tiled=True)]
    all_to_all x0 -> x1, local copies, waits for them, and re-layouts: none -> 6.51 us  [tiled_gather(): lax.all_to_all(jnp.tile(x, repeats), axis, split_axis=dim, concat_axis=di...]
  transfers between devices with their start and end apart: 3 -> 2, of which waited for: 2 -> 1; matrix products, arithmetic and copies ran while one was open for 22% -> 19% of each run, Pallas kernels for 0% -> 0%
where the time goes in v1:
time: 218 us; the launch traced here: 217 us
  local copies, waits for them, and re-layouts  63.4 us (29%)
  blocking collectives  56.8 us (26%)
  matrix products  33 us (15%)
  waiting for transfers between devices  32.8 us (15%)
  between operations  14.1 us (6%)
  other arithmetic  12.4 us (6%)
  starting transfers between devices  4.39 us (2%)
    all_to_all x1, blocking collectives, tiled_gather(): lax.all_to_all(jnp.tile(x, repeats), axis, split_axis=dim, concat_axis=di...  56.8 us
    all_gather x1, waiting for transfers between devices, shards(): gathered = lax.all_gather(block_rows[:, None], 'ctx', axis=1, tiled=True)  32.8 us
    reshape x4, local copies, waits for them, and re-layouts, shards(): vert_mask = jnp.broadcast_to(block_mask[:, None, :, None], (per_dev, BLOC...  18.8 us
    dot_general x4, matrix products, shards(): jnp.einsum('qd,kd->qk', query_head, vert_keys, preferred_element_type=jnp...  14.6 us
    unnamed x88, local copies, waits for them, and re-layouts  6.65 us
    dot_general x1, matrix products, shards(): jnp.dot(tiled_gather(attended, 'head', 1), out_weight, preferred_element_...  6.61 us
    all_to_all x1, local copies, waits for them, and re-layouts, tiled_gather(): lax.all_to_all(jnp.tile(x, repeats), axis, split_axis=dim, concat_axis=di...  6.51 us
    dot_general x4, matrix products, attend(): jnp.einsum('wojf,wjfl->wol', slash_probability, diagonal_values, preferre...  6.32 us
  transfers between devices with their start and end apart: 2, of which 1 were waited for; matrix products, arithmetic and copies ran while one was open for 19% of the time, Pallas kernels for 0%

profile of v1, /device:TPU:1, one launch (start us, length us, event | category | flops | bytes accessed | tf_op | source)
XLA Modules:
  0.0 216.9 jit_solution(16728484728419785104)
XLA Ops:
  6.5 0.8 constant_dynamic-slice_fusion
  7.5 0.9 dynamic-slice_reduce_fusion
  8.4 0.6 gather_fusion.6
  9.1 1.0 pad_maximum_fusion.1
  10.1 1.2 gather_fusion
  11.3 1.0 pad_maximum_fusion.2
  12.3 4.4 %collective-permute-start = (bf16[2,512,128]{2,1,0:T(8,128)(2,1)S(1)}, bf16[2,512,128]{2,1,0:T(8,128)(2,1)S(1)}, u32[]{:S(2)}, u32[]{:S(2)}) collective-permute-start(bf16[2,512,128]{2,1,0:T(8,128)(2,1)S(1)} %pad_maximum_fusion.2), channel_id=1, source_target_pairs={{0,8},{8,16},{16,24},{24,32},{32,40},{40,48},{48,56},{56,64},{64,7... | collective-permute-start | bytes 786440 | tf_op jit(solution)/shard_map/ppermute | solution.py:21
  16.7 0.7 fusion.89
  17.5 0.8 copy.81
  18.3 1.5 gather_fusion.5
  20.8 0.7 subtract_compare_fusion.3
  21.6 0.8 broadcast_or_fusion.3
  23.0 0.6 broadcast_in_dim.29
  23.6 4.7 %reshape.1058 = pred[512,2048]{0,1:T(32,128)(4,1)} reshape(pred[8,64,32,64]{1,0,3,2:T(8,128)(4,1)S(1)} %broadcast_in_dim.29) | data formatting | bytes 2097152 | tf_op jit(solution)/shard_map/reshape | solution.py:104
  28.4 0.7 add.293
  29.7 4.7 %reshape.1061 = pred[512,2048]{0,1:T(32,128)(4,1)} reshape(pred[8,64,32,64]{1,0,3,2:T(8,128)(4,1)S(1)} %broadcast_in_dim.33) | data formatting | bytes 2097152 | tf_op jit(solution)/shard_map/reshape | solution.py:104
  34.4 0.7 add.307
  35.2 0.6 broadcast_in_dim.34
  35.8 4.7 %reshape.1064 = pred[512,2048]{0,1:T(32,128)(4,1)} reshape(pred[8,64,32,64]{1,0,3,2:T(8,128)(4,1)S(1)} %broadcast_in_dim.34) | data formatting | bytes 2097152 | tf_op jit(solution)/shard_map/reshape | solution.py:104
  40.6 0.7 add.314
  41.3 0.6 broadcast_in_dim.35
  41.9 4.7 %reshape.1067 = pred[512,2048]{0,1:T(32,128)(4,1)} reshape(pred[8,64,32,64]{1,0,3,2:T(8,128)(4,1)S(1)} %broadcast_in_dim.35) | data formatting | bytes 2097152 | tf_op jit(solution)/shard_map/reshape | solution.py:104
  46.6 0.7 add.321
  47.3 0.7 fusion.99
  48.1 0.7 gather_fusion.1
  49.0 1.0 copy-done.9
  49.9 1.3 fusion.107
  51.3 0.7 gather_fusion.2
  52.2 1.0 copy-done.8
  53.6 0.7 reduce_max.94
  54.2 0.7 gather_fusion.3
  55.1 1.0 copy-done.7
  56.5 0.7 reduce_max.98
  57.1 1.6 gather_fusion.4
  58.8 1.3 copy.96
  60.1 1.0 copy-done.5
  61.5 32.8 %all-gather.3.cloned.1.call-done = bf16[4,64,64,128]{3,2,1,0:T(8,128)(2,1)} async-done(((bf16[4,2,64,128]{3,2,1,0:T(8,128)(2,1)}), bf16[4,64,64,128]{3,2,1,0:T(8,128)(2,1)}) %all-gather.3.cloned.1.call-update) | async-done | bytes 4194320 | tf_op jit(solution)/shard_map/all_gather | solution.py:74
  94.3 4.4 %fusion.94 = (bf16[1,64,64,128]{3,2,1,0:T(8,128)(2,1)S(1)}, bf16[1,64,64,128]{3,2,1,0:T(8,128)(2,1)}, bf16[1,64,64,128]{3,2,1,0:T(8,128)(2,1)}, bf16[1,64,64,128]{3,2,1,0:T(8,128)(2,1)}) fusion(bf16[4,64,64,128]{3,2,1,0:T(8,128)(2,1)} %all-gather.3.cloned.1.call-done), kind=kLoop, calls=%fused_computation.176 | loop fusion | bytes 8388608 | tf_op jit(solution)/shard_map/slice | solution.py:88
  98.7 0.9 fusion.95
  99.6 3.6 %fusion.106 = (f32[512]{0:T(512)S(1)}, f32[512,2048]{0,1:T(8,128)}) fusion(bf16[2048,128]{1,0:T(8,128)(2,1)S(1)} %bitcast.254, bf16[512,512]{1,0:T(8,128)(2,1)} %param.8, pred[512,2048]{0,1:T(32,128)(4,1)S(1)} %copy-done.19, s32[512]{0:T(512)S(1)} %copy-done.37, s32[2048]{0:T(1024)S(1)} %copy-done.32), kind=kOutput, calls=%fused_computation.188 | convolution fusion | flops 273677824 | bytes 5910528 | tf_op jit(solution)/shard_map/qd,kd->qk/dot_general | solution.py:95
  103.3 1.5 fusion.64
  104.8 1.7 fusion.78
  106.5 2.1 fusion.96
  108.6 3.6 %fusion.104 = (f32[512]{0:T(512)S(1)}, f32[512,2048]{0,1:T(8,128)}) fusion(bf16[2048,128]{1,0:T(8,128)(2,1)S(1)} %bitcast.255, bf16[512,512]{1,0:T(8,128)(2,1)} %param.8, pred[512,2048]{0,1:T(32,128)(4,1)S(1)} %copy-done.18, s32[512]{0:T(512)S(1)} %copy-done.37, s32[2048]{0:T(1024)S(1)} %copy-done.31), kind=kOutput, calls=%fused_computation.186 | convolution fusion | flops 273677824 | bytes 5910528 | tf_op jit(solution)/shard_map/qd,kd->qk/dot_general | solution.py:95
  112.5 2.2 %fusion.76 = f32[8,64,128,1]{2,1,3,0:T(8,128)} fusion(f32[8,64,4,64]{1,3,2,0:T(8,128)S(1)} %get-tuple-element.68, bf16[2,8,4,64,128]{4,3,2,1,0:T(8,128)(2,1)} %bitcast.236, f32[8,64]{1,0:T(8,128)S(1)} %max.47), kind=kOutput, calls=%fused_computation.70 | convolution fusion | flops 33816576 | bytes 1312768 | tf_op jit(solution)/shard_map/wojf,wjfl->wol/dot_general | solution.py:42
  114.6 2.1 fusion.97
  116.7 3.7 %fusion.102 = (f32[512]{0:T(512)S(1)}, f32[512,2048]{0,1:T(8,128)}) fusion(bf16[2048,128]{1,0:T(8,128)(2,1)S(1)} %bitcast.256, bf16[512,512]{1,0:T(8,128)(2,1)} %param.8, pred[512,2048]{0,1:T(32,128)(4,1)S(1)} %copy-done.17, s32[512]{0:T(512)S(1)} %copy-done.37, s32[2048]{0:T(1024)S(1)} %copy-done.30), kind=kOutput, calls=%fused_computation.184 | convolution fusion | flops 273677824 | bytes 5910528 | tf_op jit(solution)/shard_map/qd,kd->qk/dot_general | solution.py:95
  120.7 2.2 fusion.74
  122.9 0.9 fusion.98
  123.8 3.7 %fusion.100 = (f32[512]{0:T(512)S(1)}, f32[512,2048]{0,1:T(8,128)}) fusion(bf16[2048,128]{1,0:T(8,128)(2,1)S(1)} %bitcast.253, bf16[512,512]{1,0:T(8,128)(2,1)} %param.8, pred[512,2048]{0,1:T(32,128)(4,1)S(1)} %copy-done.16, s32[512]{0:T(512)S(1)} %copy-done.37, s32[2048]{0:T(1024)S(1)} %copy-done.29), kind=kOutput, calls=%fused_computation.182 | convolution fusion | flops 273677824 | bytes 5910528 | tf_op jit(solution)/shard_map/qd,kd->qk/dot_general | solution.py:95
  129.0 3.0 %fusion = f32[512]{0:T(512)S(1)} fusion(f32[512,2048]{0,1:T(8,128)} %get-tuple-element.70, f32[512]{0:T(512)S(1)} %max.44), kind=kLoop, calls=%fused_computation.15 | loop fusion | flops 2096640 | bytes 4198400 | tf_op jit(solution)/shard_map/reduce_sum | solution.py:34
  132.5 0.6 fusion.2
  133.1 0.6 copy-done.2
  133.8 0.6 fusion.4
  134.4 0.8 copy-done.3
  135.2 0.6 fusion.6
  135.8 0.6 copy-done
  136.4 0.8 fusion.61
  137.2 0.7 fusion.58
  138.0 0.8 fusion.55
  138.8 0.8 fusion.52
  140.2 56.8 %all_to_all.9 = bf16[512,8,512]{2,0,1:T(8,128)(2,1)} all-to-all(bf16[512,8,512]{2,0,1:T(8,128)(2,1)S(1)} %tile.2), channel_id=1, replica_groups=mesh['ctx'=32,'head'=8] {'head'}, dimensions={1} | all-to-all | bytes 8388608 | tf_op jit(solution)/shard_map/all_to_all | solution.py:15
  197.0 6.5 %copy.100 = bf16[512,8,512]{0,2,1:T(8,128)(2,1)} copy(bf16[512,8,512]{2,0,1:T(8,128)(2,1)} %all_to_all.9) | data formatting | bytes 8388608 | tf_op jit(solution)/shard_map/all_to_all | solution.py:15
  203.5 6.6 %convolution_convert_fusion = bf16[512,512]{1,0:T(8,128)(2,1)} fusion(bf16[512,4096]{0,1:T(8,128)(2,1)} %bitcast.226, bf16[4096,512]{1,0:T(8,128)(2,1)} %param.15), kind=kOutput, calls=%fused_computation.43 | convolution fusion | flops 2147745792 | bytes 8912896 | tf_op jit(solution)/shard_map/dot_general | solution.py:136
  (171 shorter events, 7.7 us)
Async XLA Ops:
  6.5 13.8 %copy-start.28 = (s32[4,32,1]{1,2,0:T(1,128)S(1)}, s32[4,32,1]{1,2,0:T(1,128)}, u32[]{:S(2)}) copy-start(s32[4,32,1]{1,2,0:T(1,128)} %param.13) | copy-start | bytes 1540
  6.5 13.3 %copy-start.35 = (s32[4,4]{1,0:T(4,128)S(1)}, s32[4,4]{1,0:T(4,128)}, u32[]{:S(2)}) copy-start(s32[4,4]{1,0:T(4,128)} %param.11) | copy-start | bytes 196
  6.5 14.1 %copy-start.36 = (s32[4,32]{1,0:T(4,128)S(1)}, s32[4,32]{1,0:T(4,128)}, u32[]{:S(2)}) copy-start(s32[4,32]{1,0:T(4,128)} %param.14) | copy-start | bytes 1540
  6.5 87.8 %all-gather.3.cloned.1.call-start = ((), (), s32[]{:S(2)}) async-start(), calls=%async_computation.1 | async-start | bytes 4325376 | tf_op jit(solution)/shard_map/all_gather | solution.py:74
  12.3 35.8 %collective-permute-start = (bf16[2,512,128]{2,1,0:T(8,128)(2,1)S(1)}, bf16[2,512,128]{2,1,0:T(8,128)(2,1)S(1)}, u32[]{:S(2)}, u32[]{:S(2)}) collective-permute-start(bf16[2,512,128]{2,1,0:T(8,128)(2,1)S(1)} %pad_maximum_fusion.2), channel_id=1, source_target_pairs={{0,8},{8,16},{16,24},{24,32},{32,40},{40,48},{48,56},{56,64},{64,7... | collective-permute-start | bytes 786440 | tf_op jit(solution)/shard_map/ppermute | solution.py:21
  35.8 11.5 %copy-start.22 = (bf16[512,512]{1,0:T(8,128)(2,1)S(1)}, bf16[512,512]{1,0:T(8,128)(2,1)}, u32[]{:S(2)}) copy-start(bf16[512,512]{1,0:T(8,128)(2,1)} %param.8) | copy-start | bytes 1572868
  35.8 12.2 %copy-start.14 = (bf16[512,128]{1,0:T(8,128)(2,1)S(1)}, bf16[512,128]{1,0:T(8,128)(2,1)}, u32[]{:S(2)}) copy-start(bf16[512,128]{1,0:T(8,128)(2,1)} %param.10) | copy-start | bytes 393220
  35.8 12.2 %copy-start.15 = (bf16[512,128]{1,0:T(8,128)(2,1)S(1)}, bf16[512,128]{1,0:T(8,128)(2,1)}, u32[]{:S(2)}) copy-start(bf16[512,128]{1,0:T(8,128)(2,1)} %param.9) | copy-start | bytes 393220
  46.6 3.3 %copy-start.27 = (pred[64,4,64]{0,2,1:T(8,128)(4,1)S(1)}, pred[64,4,64]{0,2,1:T(8,128)(4,1)}, u32[]{:S(2)}) copy-start(pred[64,4,64]{0,2,1:T(8,128)(4,1)} %get-tuple-element.21) | copy-start | bytes 49156
  46.6 3.3 %copy-start.41 = (pred[8,4]{1,0:T(8,128)(4,1)S(1)}, pred[8,4]{1,0:T(8,128)(4,1)}, u32[]{:S(2)}) copy-start(pred[8,4]{1,0:T(8,128)(4,1)} %get-tuple-element.49) | copy-start | bytes 100
  48.9 4.4 %copy-start.26 = (pred[64,4,64]{0,2,1:T(8,128)(4,1)S(1)}, pred[64,4,64]{0,2,1:T(8,128)(4,1)}, u32[]{:S(2)}) copy-start(pred[64,4,64]{0,2,1:T(8,128)(4,1)} %get-tuple-element.22) | copy-start | bytes 49156
  48.9 4.4 %copy-start.40 = (pred[8,4]{1,0:T(8,128)(4,1)S(1)}, pred[8,4]{1,0:T(8,128)(4,1)}, u32[]{:S(2)}) copy-start(pred[8,4]{1,0:T(8,128)(4,1)} %get-tuple-element.50) | copy-start | bytes 100
  49.0 1.0 copy-start.9
  52.1 4.0 %copy-start.23 = (bf16[512,128]{1,0:T(8,128)(2,1)S(1)}, bf16[512,128]{1,0:T(8,128)(2,1)}, u32[]{:S(2)}) copy-start(bf16[512,128]{1,0:T(8,128)(2,1)} %get-tuple-element.20) | copy-start | bytes 393220
  52.1 4.0 %copy-start.25 = (pred[64,4,64]{0,2,1:T(8,128)(4,1)S(1)}, pred[64,4,64]{0,2,1:T(8,128)(4,1)}, u32[]{:S(2)}) copy-start(pred[64,4,64]{0,2,1:T(8,128)(4,1)} %get-tuple-element.23) | copy-start | bytes 49156
  52.1 4.0 %copy-start.39 = (pred[8,4]{1,0:T(8,128)(4,1)S(1)}, pred[8,4]{1,0:T(8,128)(4,1)}, u32[]{:S(2)}) copy-start(pred[8,4]{1,0:T(8,128)(4,1)} %get-tuple-element.51) | copy-start | bytes 100
  52.2 1.0 copy-start.8
  55.0 6.1 %copy-start.24 = (pred[64,4,64]{0,2,1:T(8,128)(4,1)S(1)}, pred[64,4,64]{0,2,1:T(8,128)(4,1)}, u32[]{:S(2)}) copy-start(pred[64,4,64]{0,2,1:T(8,128)(4,1)} %get-tuple-element.24) | copy-start | bytes 49156
  55.0 6.1 %copy-start.38 = (pred[8,4]{1,0:T(8,128)(4,1)S(1)}, pred[8,4]{1,0:T(8,128)(4,1)}, u32[]{:S(2)}) copy-start(pred[8,4]{1,0:T(8,128)(4,1)} %get-tuple-element.52) | copy-start | bytes 100
  55.1 1.0 copy-start.7
  60.1 1.0 copy-start.5
  61.5 38.1 %copy-start.32 = (s32[2048]{0:T(1024)S(1)}, s32[2048]{0:T(1024)}, u32[]{:S(2)}) copy-start(s32[2048]{0:T(1024)} %add.293) | copy-start | bytes 24580
  61.5 38.1 %copy-start.37 = (s32[512]{0:T(512)S(1)}, s32[512]{0:T(512)}, u32[]{:S(2)}) copy-start(s32[512]{0:T(512)} %iota_add_fusion.4) | copy-start | bytes 6148
  94.3 5.3 %copy-start.19 = (pred[512,2048]{0,1:T(32,128)(4,1)S(1)}, pred[512,2048]{0,1:T(32,128)(4,1)}, u32[]{:S(2)}) copy-start(pred[512,2048]{0,1:T(32,128)(4,1)} %reshape.1058) | copy-start | bytes 3145732
  99.6 8.9 %copy-start.31 = (s32[2048]{0:T(1024)S(1)}, s32[2048]{0:T(1024)}, u32[]{:S(2)}) copy-start(s32[2048]{0:T(1024)} %add.307) | copy-start | bytes 24580
  103.3 5.3 %copy-start.18 = (pred[512,2048]{0,1:T(32,128)(4,1)S(1)}, pred[512,2048]{0,1:T(32,128)(4,1)}, u32[]{:S(2)}) copy-start(pred[512,2048]{0,1:T(32,128)(4,1)} %reshape.1061) | copy-start | bytes 3145732
  108.6 8.2 %copy-start.30 = (s32[2048]{0:T(1024)S(1)}, s32[2048]{0:T(1024)}, u32[]{:S(2)}) copy-start(s32[2048]{0:T(1024)} %add.314) | copy-start | bytes 24580
  112.3 4.5 %copy-start.17 = (pred[512,2048]{0,1:T(32,128)(4,1)S(1)}, pred[512,2048]{0,1:T(32,128)(4,1)}, u32[]{:S(2)}) copy-start(pred[512,2048]{0,1:T(32,128)(4,1)} %reshape.1064) | copy-start | bytes 3145732
  116.7 6.2 %copy-start.4 = (bf16[1,64,64,128]{3,2,1,0:T(8,128)(2,1)S(1)}, bf16[1,64,64,128]{3,2,1,0:T(8,128)(2,1)}, u32[]{:S(2)}) copy-start(bf16[1,64,64,128]{3,2,1,0:T(8,128)(2,1)} %get-tuple-element.8) | copy-start | bytes 3145732
  116.7 7.0 %copy-start.29 = (s32[2048]{0:T(1024)S(1)}, s32[2048]{0:T(1024)}, u32[]{:S(2)}) copy-start(s32[2048]{0:T(1024)} %add.321) | copy-start | bytes 24580
  120.5 3.2 %copy-start.16 = (pred[512,2048]{0,1:T(32,128)(4,1)S(1)}, pred[512,2048]{0,1:T(32,128)(4,1)}, u32[]{:S(2)}) copy-start(pred[512,2048]{0,1:T(32,128)(4,1)} %reshape.1067) | copy-start | bytes 3145732
  123.8 4.0 %copy-start.6 = (bf16[32,2,64,128]{3,2,0,1:T(8,128)(2,1)S(1)}, bf16[32,2,64,128]{3,2,0,1:T(8,128)(2,1)}, u32[]{:S(2)}) copy-start(bf16[32,2,64,128]{3,2,0,1:T(8,128)(2,1)} %copy-done.5) | copy-start | bytes 3145732
  123.8 4.6 %copy-start.33 = (f32[512]{0:T(512)S(1)}, f32[512]{0:T(512)}, u32[]{:S(2)}) copy-start(f32[512]{0:T(512)} %reduce_max.94) | copy-start | bytes 6148
  123.8 4.7 %copy-start.20 = (f32[8,64,128,1]{2,1,3,0:T(8,128)S(1)}, f32[8,64,128,1]{2,1,3,0:T(8,128)}, u32[]{:S(2)}) copy-start(f32[8,64,128,1]{2,1,3,0:T(8,128)} %fusion.76) | copy-start | bytes 786436
  123.8 4.8 %copy-start.34 = (f32[512]{0:T(512)S(1)}, f32[512]{0:T(512)}, u32[]{:S(2)}) copy-start(f32[512]{0:T(512)} %reduce_max.98) | copy-start | bytes 6148
  123.8 4.9 %copy-start.21 = (f32[8,64,128,1]{2,1,3,0:T(8,128)S(1)}, f32[8,64,128,1]{2,1,3,0:T(8,128)}, u32[]{:S(2)}) copy-start(f32[8,64,128,1]{2,1,3,0:T(8,128)} %fusion.74) | copy-start | bytes 786436
  128.9 6.9 %copy-start.10 = (bf16[32,1,1,64,128]{4,3,2,0,1:T(8,128)(2,1)S(1)}, bf16[32,1,1,64,128]{4,3,2,0,1:T(8,128)(2,1)}, u32[]{:S(2)}) copy-start(bf16[32,1,1,64,128]{4,3,2,0,1:T(8,128)(2,1)} %get-tuple-element.9) | copy-start | bytes 1572868
  129.0 3.5 %copy-start.1 = (f32[512,2048]{0,1:T(8,128)S(1)}, f32[512,2048]{0,1:T(8,128)}, u32[]{:S(2)}) copy-start(f32[512,2048]{0,1:T(8,128)} %get-tuple-element.66) | copy-start | bytes 12582916
  129.0 4.7 %copy-start.2 = (f32[512,2048]{0,1:T(8,128)S(1)}, f32[512,2048]{0,1:T(8,128)}, u32[]{:S(2)}) copy-start(f32[512,2048]{0,1:T(8,128)} %get-tuple-element.62) | copy-start | bytes 12582916
  132.5 2.7 %copy-start.3 = (f32[512,2048]{0,1:T(8,128)S(1)}, f32[512,2048]{0,1:T(8,128)}, u32[]{:S(2)}) copy-start(f32[512,2048]{0,1:T(8,128)} %get-tuple-element.58) | copy-start | bytes 12582916
  133.8 2.7 %copy-start = (f32[512,2048]{0,1:T(8,128)S(1)}, f32[512,2048]{0,1:T(8,128)}, u32[]{:S(2)}) copy-start(f32[512,2048]{0,1:T(8,128)} %get-tuple-element.70) | copy-start | bytes 12582916
  135.2 2.0 copy-start.11
  136.4 1.5 copy-start.12
  137.2 1.5 copy-start.13
Sparse Core Ops, SparseCore 0:
  11.4 82.8 all-gather.2
